TPU v7x, 32 devices: a whole 2x2x4 slice. The times are simulated.
32 devices in a mesh: gx: 8 (over z, x), gy: 4 (over y, core).
Axes of the slice: x: 2, y: 2, z: 4, core: 2. Of those that a mesh axis runs over, the one named last changes fastest.
Arguments:
- base_flow: float32 [3, 192, 32, 1024], P(None, 'gx', None, 'gy'), may hold values from -6 to 6
- adjoint: float32 [3, 192, 32, 1024], P(None, 'gx', None, 'gy'), may hold values from -6 to 6
- first_op: bfloat16 [1024, 1024], replicated, may hold values from -2 to 2
- second_op: bfloat16 [1024, 1024], replicated, may hold values from -9 to 5
Outputs:
- new_adjoint: float32 [3, 192, 32, 1024], P(None, 'gx', None, 'gy')
All inputs are finite; a program needn't handle non-finite values.
Results may differ from a plain program's by a relative error of at most 0.0025.
Values may be sent and summed in bfloat16 or wider, within the bound.
A program may use at most 128 MiB of HBM per device.

v0:
```python
import jax
import jax.numpy as jnp
from jax import lax
from jax.sharding import PartitionSpec as P

C_FIRST = (0.8, -0.2, 4.0 / 105.0, -1.0 / 280.0)
C_SECOND = (1.6, -0.2, 8.0 / 315.0, -1.0 / 560.0)
C_CENTER = -205.0 / 72.0
VISCOSITY = 0.1
STEP_WEIGHT = 0.5


def padded(cells, sides, width):
    for axis, dim in sides:
        count = lax.axis_size(axis)
        head = lax.slice_in_dim(cells, 0, width, axis=dim)
        tail = lax.slice_in_dim(cells, cells.shape[dim] - width, cells.shape[dim], axis=dim)
        cells = jnp.concatenate(
            [
                lax.ppermute(tail, axis, [(i, (i + 1) % count) for i in range(count)]),
                cells,
                lax.ppermute(head, axis, [((i + 1) % count, i) for i in range(count)]),
            ],
            axis=dim,
        )
    return cells


def first_streamwise(extended, cells):
    result = C_FIRST[0] * (extended[:, 5 : 5 + cells] - extended[:, 3 : 3 + cells])
    for offset in range(2, 5):
        result = result + C_FIRST[offset - 1] * (
            extended[:, 4 + offset : 4 + offset + cells]
            - extended[:, 4 - offset : 4 - offset + cells]
        )
    return result


def second_streamwise(extended, cells):
    result = C_CENTER * extended[:, 4 : 4 + cells]
    for offset in range(1, 5):
        result = result + C_SECOND[offset - 1] * (
            extended[:, 4 + offset : 4 + offset + cells]
            + extended[:, 4 - offset : 4 - offset + cells]
        )
    return result


def first_periodic(field, direction):
    result = C_FIRST[0] * (jnp.roll(field, -1, direction) - jnp.roll(field, 1, direction))
    for offset in range(2, 5):
        result = result + C_FIRST[offset - 1] * (
            jnp.roll(field, -offset, direction) - jnp.roll(field, offset, direction)
        )
    return result


def second_periodic(field, direction):
    result = C_CENTER * field
    for offset in range(1, 5):
        result = result + C_SECOND[offset - 1] * (
            jnp.roll(field, -offset, direction) + jnp.roll(field, offset, direction)
        )
    return result


def wall_combine(normal_vel, slope_adj, curvature, adjoint_low, slope_base):
    coupling = jnp.sum(adjoint_low * slope_base, axis=0)
    first_part = normal_vel * slope_adj[0] + VISCOSITY * curvature[0]
    middle_part = normal_vel * slope_adj[1] + VISCOSITY * curvature[1] - coupling
    last_part = normal_vel * slope_adj[2] + VISCOSITY * curvature[2]
    return jnp.stack((first_part, middle_part, last_part), 0)


def body(base_flow, adjoint, first_op, second_op):
    cells = base_flow.shape[1]
    spanwise = base_flow.shape[2]
    local_rows = base_flow.shape[3]
    groups = lax.axis_size("gy")
    total_rows = local_rows * groups
    extended_base = padded(base_flow, (("gx", 1),), 4)
    extended_adj = padded(adjoint, (("gx", 1),), 4)
    base_low = lax.optimization_barrier(base_flow.astype(jnp.bfloat16))
    adjoint_low = lax.optimization_barrier(adjoint.astype(jnp.bfloat16))
    base_blocks = base_low.reshape(3, cells, spanwise, 1, local_rows)
    adjoint_blocks = adjoint_low.reshape(3, cells, spanwise, 1, local_rows)
    first_blocks = first_op.reshape(total_rows, groups, local_rows)
    second_blocks = second_op.reshape(total_rows, groups, local_rows)
    base_lines = lax.all_to_all(base_blocks, "gy", split_axis=2, concat_axis=3, tiled=True)
    adjoint_lines = lax.all_to_all(adjoint_blocks, "gy", split_axis=2, concat_axis=3, tiled=True)
    items = base_lines.shape[1]
    span_part = base_lines.shape[2]
    slope_base = jnp.einsum(
        "fxzpk,ipk->fxzi", base_lines, first_blocks, preferred_element_type=jnp.float32
    )
    slope_adj = jnp.einsum(
        "fxzpk,ipk->fxzi", adjoint_lines, first_blocks, preferred_element_type=jnp.float32
    )
    curves = jnp.einsum(
        "fxzpk,ipk->fxzi", adjoint_lines, second_blocks, preferred_element_type=jnp.float32
    )
    normal_vel = base_lines[1].astype(jnp.float32).reshape(items, span_part, total_rows)
    adjoint_full = adjoint_lines.astype(jnp.float32).reshape(3, items, span_part, total_rows)
    wall_part = wall_combine(normal_vel, slope_adj, curves, adjoint_full, slope_base)
    returned = lax.all_to_all(
        wall_part.reshape(
            wall_part.shape[0], wall_part.shape[1], wall_part.shape[2], groups, local_rows
        ),
        "gy",
        split_axis=3,
        concat_axis=2,
        tiled=True,
    )
    dx_base = first_streamwise(extended_base, cells)
    dz_base = first_periodic(base_flow, 2)
    dx_adj = first_streamwise(extended_adj, cells)
    dxx_adj = second_streamwise(extended_adj, cells)
    dz_adj = first_periodic(adjoint, 2)
    dzz_adj = second_periodic(adjoint, 2)
    carried = (
        base_flow[0][None] * dx_adj + base_flow[2][None] * dz_adj + VISCOSITY * (dxx_adj + dzz_adj)
    )
    first_coupling = jnp.sum(adjoint * dx_base, axis=0)
    last_coupling = jnp.sum(adjoint * dz_base, axis=0)
    tendency = jnp.stack((carried[0] - first_coupling, carried[1], carried[2] - last_coupling), 0)
    field_shape = (3, cells, spanwise, local_rows)
    wall_part = returned.reshape(field_shape)
    updated = adjoint + STEP_WEIGHT * (tendency + wall_part)
    wall_index = lax.axis_index("gy") * local_rows + jnp.arange(local_rows, dtype=jnp.int32)
    interior = (wall_index > 0) & (wall_index < total_rows - 1)
    return jnp.where(interior, updated, jnp.float32(0.0))


def solution(mesh):
    return jax.shard_map(
        body,
        mesh=mesh,
        in_specs=(P(None, "gx", None, "gy"), P(None, "gx", None, "gy"), P(), P()),
        out_specs=P(None, "gx", None, "gy"),
        check_vma=False,
    )
```

profile of v0, /device:TPU:0, one launch (start us, length us, event | category | flops | bytes accessed | tf_op | source)
XLA Modules:
  0.0 132.8 jit_solution(5239181309676148411)
XLA Ops:
  0.0 2.2 %fusion.57 = (f32[3,4,32,256]{3,2,1,0:T(8,128)}, f32[3,4,32,256]{3,2,1,0:T(8,128)}) fusion(f32[3,24,32,256]{3,2,1,0:T(8,128)} %param.5), kind=kLoop, calls=%fused_computation.91 | loop fusion | bytes 1572864 | tf_op jit(solution)/shard_map/slice | solution.py:16
  2.2 2.9 %collective-permute-start.1 = (f32[3,4,32,256]{3,2,1,0:T(8,128)}, f32[3,4,32,256]{3,2,1,0:T(8,128)}, u32[]{:S(2)}, u32[]{:S(2)}) collective-permute-start(f32[3,4,32,256]{3,2,1,0:T(8,128)} %get-tuple-element.34), channel_id=1, source_target_pairs={{0,4},{4,8},{8,12},{12,16},{16,20},{20,24},{24,28},{28,0},{1,5},{5... | collective-permute-start | bytes 1179656 | tf_op jit(solution)/shard_map/ppermute | solution.py:20
  5.2 3.0 %collective-permute-start = (f32[3,4,32,256]{3,2,1,0:T(8,128)}, f32[3,4,32,256]{3,2,1,0:T(8,128)}, u32[]{:S(2)}, u32[]{:S(2)}) collective-permute-start(f32[3,4,32,256]{3,2,1,0:T(8,128)} %get-tuple-element.33), channel_id=1, source_target_pairs={{4,0},{8,4},{12,8},{16,12},{20,16},{24,20},{28,24},{0,28},{5,1},{9... | collective-permute-start | bytes 1179656 | tf_op jit(solution)/shard_map/ppermute | solution.py:22
  8.2 2.1 %fusion.48 = (f32[3,4,32,256]{3,2,1,0:T(8,128)}, f32[3,4,32,256]{3,2,1,0:T(8,128)}) fusion(f32[3,24,32,256]{3,2,1,0:T(8,128)} %param.4), kind=kLoop, calls=%fused_computation.82 | loop fusion | bytes 1572864 | tf_op jit(solution)/shard_map/slice | solution.py:16
  10.3 0.0 collective-permute-start.3
  10.3 4.7 %collective-permute-start.2 = (f32[3,4,32,256]{3,2,1,0:T(8,128)}, f32[3,4,32,256]{3,2,1,0:T(8,128)}, u32[]{:S(2)}, u32[]{:S(2)}) collective-permute-start(f32[3,4,32,256]{3,2,1,0:T(8,128)} %get-tuple-element.11), channel_id=1, source_target_pairs={{4,0},{8,4},{12,8},{16,12},{20,16},{24,20},{28,24},{0,28},{5,1},{9... | collective-permute-start | bytes 1179656 | tf_op jit(solution)/shard_map/ppermute | solution.py:22
  15.0 0.0 copy-done.1
  15.0 2.3 %copy.71 = bf16[3,24,32,256]{3,1,0,2:T(8,128)(2,1)} copy(f32[3,24,32,256]{3,2,1,0:T(8,128)S(1)} %copy-done.1) | data formatting | bytes 3538944 | tf_op args[0]
  17.3 3.5 %all-to-all-start = ((bf16[3,24,32,1,256]{4,1,0,3,2:T(8,128)(2,1)}), bf16[3,24,32,1,256]{4,1,0,3,2:T(8,128)(2,1)S(1)}, u32[]{:S(2)}, u32[]{:S(2)}) async-start(bf16[3,24,32,1,256]{4,1,0,3,2:T(8,128)(2,1)} %bitcast.4), calls=%async_computation | async-start | bytes 2359296 | tf_op jit(solution)/shard_map/all_to_all | solution.py:89
  20.9 0.0 copy-done
  20.9 2.7 %fusion.58 = (f32[3,24,31,256]{3,2,1,0:T(8,128)}, f32[3,24,31,256]{3,2,1,0:T(8,128)}) fusion(f32[3,24,32,256]{3,2,1,0:T(8,128)S(1)} %copy-done), kind=kLoop, calls=%fused_computation.92 | loop fusion | bytes 9142272 | tf_op jit(solution)/shard_map/jit(_roll_static)/slice | solution.py:50
  23.6 2.7 %fusion.60 = (f32[3,24,30,256]{3,2,1,0:T(8,128)}, f32[3,24,30,256]{3,2,1,0:T(8,128)}) fusion(f32[3,24,32,256]{3,2,1,0:T(8,128)S(1)} %copy-done), kind=kLoop, calls=%fused_computation.94 | loop fusion | bytes 8847360 | tf_op jit(solution)/shard_map/jit(_roll_static)/slice | solution.py:53
  26.2 2.7 %fusion.62 = (f32[3,24,29,256]{3,2,1,0:T(8,128)}, f32[3,24,29,256]{3,2,1,0:T(8,128)}) fusion(f32[3,24,32,256]{3,2,1,0:T(8,128)S(1)} %copy-done), kind=kLoop, calls=%fused_computation.96 | loop fusion | bytes 8552448 | tf_op jit(solution)/shard_map/jit(_roll_static)/slice | solution.py:53
  29.0 2.7 %fusion.64 = (f32[3,24,28,256]{3,2,1,0:T(8,128)}, f32[3,24,28,256]{3,2,1,0:T(8,128)}) fusion(f32[3,24,32,256]{3,2,1,0:T(8,128)S(1)} %copy-done), kind=kLoop, calls=%fused_computation.98 | loop fusion | bytes 8257536 | tf_op jit(solution)/shard_map/jit(_roll_static)/slice | solution.py:53
  31.7 0.9 fusion.63
  32.6 0.9 fusion.65
  33.6 0.8 fusion.61
  34.4 0.0 copy-done.2
  34.4 0.6 fusion.50
  35.0 0.6 fusion.52
  35.6 0.6 fusion.54
  36.3 0.6 fusion.56
  36.9 0.1 fusion.49
  37.0 0.1 fusion.51
  37.1 0.1 fusion.53
  37.3 0.1 fusion.55
  37.4 4.6 %fusion.14 = f32[24,32,256]{2,1,0:T(8,128)} fusion(f32[3,24,32,256]{3,2,1,0:T(8,128)S(1)} %copy-done, f32[3,24,1,256]{3,2,1,0:T(1,128)S(1)} %get-tuple-element.28, f32[3,24,31,256]{3,2,1,0:T(8,128)S(1)} %get-tuple-element.30, f32[3,24,31,256]{3,2,1,0:T(8,128)S(1)} %get-tuple-element.29, f32[3,24,1,256]{3,2,1,0:T(1,128)S(1)} %get-tuple-element.27, ...), kind=kLoop, calls=%fused_computation.27 | loop fusion | flops 12189696 | bytes 22020096 | tf_op jit(solution)/shard_map/reduce_sum | solution.py:124
  42.0 0.8 fusion.59
  42.7 2.7 %slice_bitcast_fusion.1 = (f32[24,32,256]{2,1,0:T(8,128)}, f32[24,32,256]{2,1,0:T(8,128)}) fusion(f32[3,24,32,256]{3,2,1,0:T(8,128)} %param.4), kind=kLoop, calls=%fused_computation.70 | loop fusion | bytes 3145728 | tf_op jit(solution)/shard_map/mul | solution.py:121
  45.4 2.3 %copy.70 = bf16[3,24,32,256]{3,1,0,2:T(8,128)(2,1)} copy(f32[3,24,32,256]{3,2,1,0:T(8,128)S(1)} %copy-done) | data formatting | bytes 3538944 | tf_op args[1]
  47.7 4.5 %reshape.47 = bf16[1024,4,256]{2,1,0:T(4,128)(2,1)} reshape(bf16[1024,1024]{1,0:T(8,128)(2,1)} %param.6) | data formatting | bytes 4194304 | tf_op jit(solution)/shard_map/reshape | solution.py:87
  52.2 4.5 %reshape.48 = bf16[1024,4,256]{2,1,0:T(4,128)(2,1)} reshape(bf16[1024,1024]{1,0:T(8,128)(2,1)} %param.7) | data formatting | bytes 4194304 | tf_op jit(solution)/shard_map/reshape | solution.py:88
  56.7 0.0 collective-permute-done.1
  56.7 1.8 %constant_dynamic-update-slice_fusion.3 = f32[3,28,32,256]{3,2,1,0:T(8,128)} fusion(f32[3,4,32,256]{3,2,1,0:T(8,128)} %collective-permute-done.1), kind=kLoop, calls=%fused_computation.74 | loop fusion | bytes 786432
  58.5 2.8 %constant_dynamic-update-slice_fusion.1 = (f32[3,28,32,256]{3,2,1,0:T(8,128)}, f32[3,28,32,256]{3,2,1,0:T(8,128)}) fusion(f32[3,24,32,256]{3,2,1,0:T(8,128)S(1)} %copy-done, f32[3,28,32,256]{3,2,1,0:T(8,128)} %constant_dynamic-update-slice_fusion.3), kind=kLoop, calls=%fused_computation.72 | loop fusion | bytes 7077888
  61.3 0.0 collective-permute-done.3
  61.3 1.8 %constant_dynamic-update-slice_fusion.7 = f32[3,28,32,256]{3,2,1,0:T(8,128)} fusion(f32[3,4,32,256]{3,2,1,0:T(8,128)} %collective-permute-done.3), kind=kLoop, calls=%fused_computation.78 | loop fusion | bytes 786432
  63.1 0.0 all-to-all-done
  63.1 4.5 %all-to-all-start.1 = ((bf16[3,24,32,1,256]{4,1,0,3,2:T(8,128)(2,1)}), bf16[3,24,32,1,256]{4,1,0,3,2:T(8,128)(2,1)}, u32[]{:S(2)}, u32[]{:S(2)}) async-start(bf16[3,24,32,1,256]{4,1,0,3,2:T(8,128)(2,1)} %bitcast.8), calls=%async_computation.1 | async-start | bytes 2359296 | tf_op jit(solution)/shard_map/all_to_all | solution.py:90
  67.6 3.6 %constant_dynamic-update-slice_fusion.5 = (f32[3,28,32,256]{3,2,1,0:T(8,128)S(1)}, f32[3,28,32,256]{3,2,1,0:T(8,128)}) fusion(f32[3,24,32,256]{3,2,1,0:T(8,128)} %param.4, f32[3,28,32,256]{3,2,1,0:T(8,128)} %constant_dynamic-update-slice_fusion.7), kind=kLoop, calls=%fused_computation.76 | loop fusion | bytes 7077888
  71.2 0.0 collective-permute-done
  71.2 1.8 %constant_dynamic-update-slice_fusion = f32[3,28,32,256]{3,2,1,0:T(8,128)} fusion(f32[3,28,32,256]{3,2,1,0:T(8,128)} %get-tuple-element.35, f32[3,4,32,256]{3,2,1,0:T(8,128)} %collective-permute-done), kind=kLoop, calls=%fused_computation.71 | loop fusion | bytes 786432 | tf_op jit(solution)/shard_map/concatenate | solution.py:18
  73.0 0.0 collective-permute-done.2
  73.0 1.0 constant_dynamic-update-slice_fusion.4
  74.0 6.6 %fusion.3 = f32[24,32,256]{2,1,0:T(8,128)} fusion(f32[3,24,32,256]{3,2,1,0:T(8,128)S(1)} %copy-done, f32[3,28,32,256]{3,2,1,0:T(8,128)} %get-tuple-element.14, f32[3,28,32,256]{3,2,1,0:T(8,128)S(1)} %constant_dynamic-update-slice_fusion.4), kind=kLoop, calls=%fused_computation.4 | loop fusion | flops 7471104 | bytes 22020096 | tf_op jit(solution)/shard_map/reduce_sum | solution.py:123
  80.7 0.3 copy.72
  81.0 0.8 slice.332
  81.7 1.8 %all-to-all-done.1 = bf16[3,24,32,1,256]{4,1,0,3,2:T(8,128)(2,1)} async-done(((bf16[3,24,32,1,256]{4,1,0,3,2:T(8,128)(2,1)}), bf16[3,24,32,1,256]{4,1,0,3,2:T(8,128)(2,1)}, u32[]{:S(2)}, u32[]{:S(2)}) %all-to-all-start.1) | async-done | bytes 1179680 | tf_op jit(solution)/shard_map/all_to_all | solution.py:90
  83.5 1.7 %copy.21 = bf16[3,24,32,1,256]{4,2,1,0,3:T(8,128)(2,1)S(1)} copy(bf16[3,24,32,1,256]{4,1,0,3,2:T(8,128)(2,1)} %all-to-all-done.1) | data formatting | bytes 2359296 | tf_op jit(solution)/shard_map/all_to_all | solution.py:90
  85.2 0.2 copy-done.7
  85.4 2.7 %fusion.28 = f32[3,24,8,1024]{3,2,1,0:T(8,128)S(1)} fusion(bf16[1024,4,256,1,1]{2,1,0,4,3:T(4,128)(2,1)S(1)} %bitcast.63, bf16[3,24,32,1,256]{4,1,0,3,2:T(8,128)(2,1)} %all-to-all-done.1), kind=kOutput, calls=%fused_computation.50 | convolution fusion | flops 1207959552 | bytes 5636096 | tf_op jit(solution)/shard_map/fxzpk,ipk->fxzi/dot_general | solution.py:96
  88.1 0.0 copy-start.6
  88.1 1.5 %fusion.21 = f32[24,8,1024]{2,1,0:T(8,128)S(1)} fusion(bf16[3,24,8,1024]{3,2,1,0:T(8,128)(2,1)S(1)} %bitcast.66, bf16[1024,4,256,1,1]{2,1,0,4,3:T(4,128)(2,1)S(1)} %bitcast.64, bf16[3,24,32,1,256]{4,1,0,3,2:T(8,128)(2,1)S(1)} %all-to-all-done), kind=kOutput, calls=%fused_computation.40 | convolution fusion | flops 1209532416 | bytes 5242880 | tf_op jit(solution)/shard_map/fxzpk,ipk->fxzi/dot_general | solution.py:93
  89.6 0.1 copy-done.6
  89.7 2.7 %fusion.31 = f32[3,24,8,1024]{3,2,1,0:T(8,128)S(1)} fusion(bf16[1024,4,256,1,1]{2,1,0,4,3:T(4,128)(2,1)S(1)} %bitcast.62, bf16[3,24,32,1,256]{4,1,0,3,2:T(8,128)(2,1)} %all-to-all-done.1), kind=kOutput, calls=%fused_computation.51 | convolution fusion | flops 1207959552 | bytes 5636096 | tf_op jit(solution)/shard_map/fxzpk,ipk->fxzi/dot_general | solution.py:99
  92.5 0.0 copy-done.8
  92.5 0.9 fusion.42
  93.4 0.2 pad_maximum_fusion.8
  93.5 1.7 %copy.41 = f32[3,24,8,4,256]{4,2,1,0,3:T(8,128)} copy(f32[3,24,8,4,256]{4,2,3,1,0:T(8,128)S(1)} %pad_maximum_fusion.8) | data formatting | bytes 4718592 | tf_op jit(solution)/shard_map/stack | solution.py:72
  95.2 4.6 %all-to-all-start.2 = ((f32[3,24,8,4,256]{4,2,1,0,3:T(8,128)}), f32[3,24,8,4,256]{4,2,1,0,3:T(8,128)}, u32[]{:S(2)}, u32[]{:S(2)}) async-start(f32[3,24,8,4,256]{4,2,1,0,3:T(8,128)} %copy.41), calls=%async_computation.2 | async-start | bytes 4718592 | tf_op jit(solution)/shard_map/all_to_all | solution.py:105
  99.9 15.3 %multiply_add_fusion = f32[3,24,32,256]{3,2,1,0:T(8,128)S(1)} fusion(f32[3,24,32,256]{3,2,1,0:T(8,128)S(1)} %copy-done, f32[3,24,28,256]{3,2,1,0:T(8,128)} %get-tuple-element.50, f32[3,24,4,256]{3,2,1,0:T(4,128)} %get-tuple-element.52, f32[3,24,4,256]{3,2,1,0:T(4,128)} %get-tuple-element.51, f32[3,24,28,256]{3,2,1,0:T(8,128)} %get-tuple-element.49, ...), kind=kLoop, calls=%fused_computation.43 | loop fusion | flops 35979264 | bytes 44040192 | tf_op jit(solution)/shard_map/add | solution.py:121
  115.2 1.5 %slice_subtract_fusion.5 = (f32[1,24,32,256]{3,2,1,0:T(8,128)S(1)}, f32[1,24,32,256]{3,2,1,0:T(8,128)}, f32[1,24,32,256]{3,2,1,0:T(8,128)}) fusion(f32[3,24,32,256]{3,2,1,0:T(8,128)S(1)} %multiply_add_fusion, f32[24,32,256]{2,1,0:T(8,128)S(1)} %copy-done.4, f32[24,32,256]{2,1,0:T(8,128)S(1)} %copy-done.3), kind=kLoop, calls=%fused_computation.68 | loop fusion | flops 393216 | bytes 6291456 | tf_op jit(solution)/shard_map/sub | solution.py:125
  116.7 11.7 %all-to-all-done.2 = f32[3,24,8,4,256]{4,2,1,0,3:T(8,128)} async-done(((f32[3,24,8,4,256]{4,2,1,0,3:T(8,128)}), f32[3,24,8,4,256]{4,2,1,0,3:T(8,128)}, u32[]{:S(2)}, u32[]{:S(2)}) %all-to-all-start.2) | async-done | bytes 2359328 | tf_op jit(solution)/shard_map/all_to_all | solution.py:105
  128.4 4.3 %fusion.20 = f32[3,24,32,256]{3,2,1,0:T(8,128)} fusion(f32[3,24,32,256]{3,2,1,0:T(8,128)S(1)} %copy-done, f32[1,24,32,256]{3,2,1,0:T(8,128)} %get-tuple-element.9, f32[1,24,32,256]{3,2,1,0:T(8,128)} %get-tuple-element.10, f32[1,24,32,256]{3,2,1,0:T(8,128)S(1)} %get-tuple-element.8, f32[3,24,8,4,256]{4,2,1,0,3:T(8,128)} %all-to-all-done.2, ...), kind=kLoop, calls=%fused_computation.37 | loop fusion | flops 3538944 | bytes 9437440 | tf_op jit(solution)/shard_map/jit(_where)/select_n | solution.py:131
  (16 shorter events, 0.0 us)
Async XLA Ops:
  0.0 15.0 %copy-start.1 = (f32[3,24,32,256]{3,2,1,0:T(8,128)S(1)}, f32[3,24,32,256]{3,2,1,0:T(8,128)}, u32[]{:S(2)}) copy-start(f32[3,24,32,256]{3,2,1,0:T(8,128)} %param.4) | copy-start | bytes 7077892
  2.2 54.5 %collective-permute-start.1 = (f32[3,4,32,256]{3,2,1,0:T(8,128)}, f32[3,4,32,256]{3,2,1,0:T(8,128)}, u32[]{:S(2)}, u32[]{:S(2)}) collective-permute-start(f32[3,4,32,256]{3,2,1,0:T(8,128)} %get-tuple-element.34), channel_id=1, source_target_pairs={{0,4},{4,8},{8,12},{12,16},{16,20},{20,24},{24,28},{28,0},{1,5},{5... | collective-permute-start | bytes 1179656 | tf_op jit(solution)/shard_map/ppermute | solution.py:20
  5.2 66.1 %collective-permute-start = (f32[3,4,32,256]{3,2,1,0:T(8,128)}, f32[3,4,32,256]{3,2,1,0:T(8,128)}, u32[]{:S(2)}, u32[]{:S(2)}) collective-permute-start(f32[3,4,32,256]{3,2,1,0:T(8,128)} %get-tuple-element.33), channel_id=1, source_target_pairs={{4,0},{8,4},{12,8},{16,12},{20,16},{24,20},{28,24},{0,28},{5,1},{9... | collective-permute-start | bytes 1179656 | tf_op jit(solution)/shard_map/ppermute | solution.py:22
  10.3 51.0 %collective-permute-start.3 = (f32[3,4,32,256]{3,2,1,0:T(8,128)}, f32[3,4,32,256]{3,2,1,0:T(8,128)}, u32[]{:S(2)}, u32[]{:S(2)}) collective-permute-start(f32[3,4,32,256]{3,2,1,0:T(8,128)} %get-tuple-element.12), channel_id=1, source_target_pairs={{0,4},{4,8},{8,12},{12,16},{16,20},{20,24},{24,28},{28,0},{1,5},{5... | collective-permute-start | bytes 1179656 | tf_op jit(solution)/shard_map/ppermute | solution.py:20
  10.3 10.6 %copy-start = (f32[3,24,32,256]{3,2,1,0:T(8,128)S(1)}, f32[3,24,32,256]{3,2,1,0:T(8,128)}, u32[]{:S(2)}) copy-start(f32[3,24,32,256]{3,2,1,0:T(8,128)} %param.5) | copy-start | bytes 7077892
  10.3 62.7 %collective-permute-start.2 = (f32[3,4,32,256]{3,2,1,0:T(8,128)}, f32[3,4,32,256]{3,2,1,0:T(8,128)}, u32[]{:S(2)}, u32[]{:S(2)}) collective-permute-start(f32[3,4,32,256]{3,2,1,0:T(8,128)} %get-tuple-element.11), channel_id=1, source_target_pairs={{4,0},{8,4},{12,8},{16,12},{20,16},{24,20},{28,24},{0,28},{5,1},{9... | collective-permute-start | bytes 1179656 | tf_op jit(solution)/shard_map/ppermute | solution.py:22
  17.3 45.8 %all-to-all-start = ((bf16[3,24,32,1,256]{4,1,0,3,2:T(8,128)(2,1)}), bf16[3,24,32,1,256]{4,1,0,3,2:T(8,128)(2,1)S(1)}, u32[]{:S(2)}, u32[]{:S(2)}) async-start(bf16[3,24,32,1,256]{4,1,0,3,2:T(8,128)(2,1)} %bitcast.4), calls=%async_computation | async-start | bytes 2359296 | tf_op jit(solution)/shard_map/all_to_all | solution.py:89
  31.7 2.7 %copy-start.2 = (f32[3,24,32,256]{3,2,1,0:T(8,128)S(1)}, f32[3,24,32,256]{3,2,1,0:T(8,128)}, u32[]{:S(2)}) copy-start(f32[3,24,32,256]{3,2,1,0:T(8,128)} %param.4) | copy-start | bytes 7077892
  63.1 20.3 %all-to-all-start.1 = ((bf16[3,24,32,1,256]{4,1,0,3,2:T(8,128)(2,1)}), bf16[3,24,32,1,256]{4,1,0,3,2:T(8,128)(2,1)}, u32[]{:S(2)}, u32[]{:S(2)}) async-start(bf16[3,24,32,1,256]{4,1,0,3,2:T(8,128)(2,1)} %bitcast.8), calls=%async_computation.1 | async-start | bytes 2359296 | tf_op jit(solution)/shard_map/all_to_all | solution.py:90
  83.5 1.9 %copy-start.7 = (bf16[1024,4,256]{2,1,0:T(4,128)(2,1)S(1)}, bf16[1024,4,256]{2,1,0:T(4,128)(2,1)}, u32[]{:S(2)}) copy-start(bf16[1024,4,256]{2,1,0:T(4,128)(2,1)} %reshape.47) | copy-start | bytes 6291460
  88.1 1.6 %copy-start.6 = (bf16[1024,4,256]{2,1,0:T(4,128)(2,1)S(1)}, bf16[1024,4,256]{2,1,0:T(4,128)(2,1)}, u32[]{:S(2)}) copy-start(bf16[1024,4,256]{2,1,0:T(4,128)(2,1)} %reshape.48) | copy-start | bytes 6291460
  89.7 2.8 %copy-start.8 = (bf16[1,24,8,4,1,256]{5,2,3,1,0,4:T(8,128)(2,1)S(1)}, bf16[1,24,8,4,1,256]{5,2,3,1,0,4:T(8,128)(2,1)}, u32[]{:S(2)}) copy-start(bf16[1,24,8,4,1,256]{5,2,3,1,0,4:T(8,128)(2,1)} %slice.332) | copy-start | bytes 1179652
  95.2 4.6 %copy-start.5 = (f32[24,32,256]{2,1,0:T(8,128)S(1)}, f32[24,32,256]{2,1,0:T(8,128)}, u32[]{:S(2)}) copy-start(f32[24,32,256]{2,1,0:T(8,128)} %get-tuple-element.31) | copy-start | bytes 2359300
  95.2 4.7 %copy-start.9 = (f32[3,24,3,256]{3,2,1,0:T(4,128)S(1)}, f32[3,24,3,256]{3,2,1,0:T(4,128)}, u32[]{:S(2)}) copy-start(f32[3,24,3,256]{3,2,1,0:T(4,128)} %get-tuple-element.47) | copy-start | bytes 663556
  95.2 4.7 %copy-start.10 = (f32[3,24,1,256]{3,2,1,0:T(1,128)S(1)}, f32[3,24,1,256]{3,2,1,0:T(1,128)}, u32[]{:S(2)}) copy-start(f32[3,24,1,256]{3,2,1,0:T(1,128)} %get-tuple-element.39) | copy-start | bytes 221188
  95.2 33.2 %all-to-all-start.2 = ((f32[3,24,8,4,256]{4,2,1,0,3:T(8,128)}), f32[3,24,8,4,256]{4,2,1,0,3:T(8,128)}, u32[]{:S(2)}, u32[]{:S(2)}) async-start(f32[3,24,8,4,256]{4,2,1,0,3:T(8,128)} %copy.41), calls=%async_computation.2 | async-start | bytes 4718592 | tf_op jit(solution)/shard_map/all_to_all | solution.py:105
  99.9 15.3 %copy-start.3 = (f32[24,32,256]{2,1,0:T(8,128)S(1)}, f32[24,32,256]{2,1,0:T(8,128)}, u32[]{:S(2)}) copy-start(f32[24,32,256]{2,1,0:T(8,128)} %fusion.14) | copy-start | bytes 2359300
  99.9 15.3 %copy-start.4 = (f32[24,32,256]{2,1,0:T(8,128)S(1)}, f32[24,32,256]{2,1,0:T(8,128)}, u32[]{:S(2)}) copy-start(f32[24,32,256]{2,1,0:T(8,128)} %fusion.3) | copy-start | bytes 2359300
where the time goes:
time: 134 us; the launch traced here: 133 us
  local copies, waits for them, and re-layouts  55.4 us (41%)
  other arithmetic  33.4 us (25%)
  starting transfers between devices  23.3 us (17%)
  waiting for transfers between devices  13.5 us (10%)
  matrix products  6.92 us (5%)
    add x1, other arithmetic, body(): base_flow[0][None] * dx_adj + base_flow[2][None] * dz_adj  15.3 us
    unnamed x28, local copies, waits for them, and re-layouts  15 us
    all_to_all x1, waiting for transfers between devices, body(): lax.all_to_all(wall_part.reshape(wall_part.shape[0], wall_part.shape[1],...  11.7 us
    slice x6, local copies, waits for them, and re-layouts, first_periodic(): jnp.roll(field, -offset, direction) - jnp.roll(field, offset, direction)  10.8 us
    ppermute x2, starting transfers between devices, padded(): lax.ppermute(head, axis, [((i + 1) % count, i) for i in range(count)])  7.76 us
    reduce_sum x1, other arithmetic, body(): first_coupling = jnp.sum(adjoint * dx_base, axis=0)  6.63 us
    all_to_all x1, starting transfers between devices, body(): lax.all_to_all(wall_part.reshape(wall_part.shape[0], wall_part.shape[1],...  4.63 us
    reduce_sum x1, other arithmetic, body(): last_coupling = jnp.sum(adjoint * dz_base, axis=0)  4.6 us
  transfers between devices with their start and end apart: 7, of which 2 were waited for; matrix products, arithmetic and copies ran while one was open for 58% of the time, Pallas kernels for 0%

commit v1 on v0

v1 whole, which is shorter than its diff:
```python
import functools

import jax
import jax.numpy as jnp
from jax import lax
from jax.experimental import pallas as pl
from jax.experimental.pallas import tpu as pltpu
from jax.sharding import PartitionSpec as P

C_FIRST = (0.8, -0.2, 4.0 / 105.0, -1.0 / 280.0)
C_SECOND = (1.6, -0.2, 8.0 / 315.0, -1.0 / 560.0)
C_CENTER = -205.0 / 72.0
VISCOSITY = 0.1
STEP_WEIGHT = 0.5
MESH = pl.DeviceIdType.MESH
WIDTH = 4
LANES = 128


def kernel(
    groups,
    ring,
    chunks,
    base_hbm,
    adjoint_hbm,
    first_hbm,
    second_hbm,
    out_ref,
    ext,
    low,
    lines,
    halo,
    first,
    second,
    back_out,
    back_in,
    in_sem,
    own_sem,
    halo_send,
    halo_recv,
    line_send,
    line_recv,
    back_send,
    back_recv,
):
    cells, span, rows = low.shape[1], low.shape[2], low.shape[3]
    share = cells // groups
    step = share // chunks
    me = lax.axis_index("gy")
    here = lax.axis_index("gx")
    right = lax.rem(here + 1, ring)
    left = lax.rem(here + ring - 1, ring)
    order = [2, 1, 3] if groups == 4 else list(range(1, groups))
    peers = {d: lax.rem(me + d, groups) for d in range(groups)}

    loads = [
        pltpu.make_async_copy(base_hbm, ext.at[0:3, WIDTH : WIDTH + cells], in_sem.at[0]),
        pltpu.make_async_copy(adjoint_hbm, ext.at[3:6, WIDTH : WIDTH + cells], in_sem.at[1]),
        pltpu.make_async_copy(first_hbm, first, in_sem.at[2]),
        pltpu.make_async_copy(second_hbm, second, in_sem.at[3]),
    ]
    for load in loads:
        load.start()

    barrier = pltpu.get_barrier_semaphore()
    for d in order:
        pl.semaphore_signal(barrier, inc=1, device_id={"gy": peers[d]}, device_id_type=MESH)
    for side in (left, right):
        pl.semaphore_signal(barrier, inc=1, device_id={"gx": side}, device_id_type=MESH)

    loads[0].wait()
    loads[1].wait()

    def cast(x, carry):
        low[:, pl.ds(x, 1)] = ext[:, pl.ds(x + WIDTH, 1)].astype(jnp.bfloat16)
        return carry

    lax.fori_loop(0, cells, cast, 0)

    pl.semaphore_wait(barrier, groups + 1)

    mine = pl.ds(pl.multiple_of(me * rows, rows), rows)

    def line_copy(c, d):
        return pltpu.make_async_remote_copy(
            src_ref=low.at[:, pl.ds(peers[d] * share + c * step, step)],
            dst_ref=lines.at[c, :, :, :, mine],
            send_sem=line_send.at[c, d],
            recv_sem=line_recv.at[c, d],
            device_id={"gy": peers[d]},
            device_id_type=MESH,
        )

    def own_copy(c):
        return pltpu.make_async_copy(
            low.at[:, pl.ds(me * share + c * step, step)],
            lines.at[c, :, :, :, mine],
            own_sem.at[c],
        )

    def back_copy(c, d):
        return pltpu.make_async_remote_copy(
            src_ref=back_out.at[c, d],
            dst_ref=back_in.at[c, me],
            send_sem=back_send.at[c, d],
            recv_sem=back_recv.at[c, d],
            device_id={"gy": peers[d]},
            device_id_type=MESH,
        )

    to_right = pltpu.make_async_remote_copy(
        src_ref=low.at[:, cells - WIDTH : cells],
        dst_ref=halo.at[0],
        send_sem=halo_send.at[0],
        recv_sem=halo_recv.at[0],
        device_id={"gx": right},
        device_id_type=MESH,
    )
    to_left = pltpu.make_async_remote_copy(
        src_ref=low.at[:, 0:WIDTH],
        dst_ref=halo.at[1],
        send_sem=halo_send.at[1],
        recv_sem=halo_recv.at[1],
        device_id={"gx": left},
        device_id_type=MESH,
    )
    for d in order:
        line_copy(0, d).start()
    to_right.start()
    to_left.start()
    for c in range(1, chunks):
        for d in order:
            line_copy(c, d).start()
    for c in range(chunks):
        own_copy(c).start()

    def derive(x, carry):
        for half in range(rows // LANES):
            cols = slice(half * LANES, (half + 1) * LANES)

            def plane(f, offset):
                return ext[f, x + (WIDTH + offset), :, cols]

            stream = plane(0, 0)
            across = plane(2, 0)
            couple_x = None
            couple_z = None
            parts = []
            for j in range(3):
                adj = plane(3 + j, 0)
                slope_x = None
                curve = (2.0 * C_CENTER) * adj
                slope_z = None
                base_x = None
                base_z = None
                field = plane(j, 0)
                for k in range(1, WIDTH + 1):
                    a_up, a_down = plane(3 + j, k), plane(3 + j, -k)
                    z_up = pltpu.roll(adj, span - k, 0)
                    z_down = pltpu.roll(adj, k, 0)
                    dx = C_FIRST[k - 1] * (a_up - a_down)
                    dz = C_FIRST[k - 1] * (z_up - z_down)
                    curve = curve + C_SECOND[k - 1] * ((a_up + a_down) + (z_up + z_down))
                    bx = C_FIRST[k - 1] * (plane(j, k) - plane(j, -k))
                    bz = C_FIRST[k - 1] * (
                        pltpu.roll(field, span - k, 0) - pltpu.roll(field, k, 0)
                    )
                    slope_x = dx if slope_x is None else slope_x + dx
                    slope_z = dz if slope_z is None else slope_z + dz
                    base_x = bx if base_x is None else base_x + bx
                    base_z = bz if base_z is None else base_z + bz
                base_x, base_z = adj * base_x, adj * base_z
                couple_x = base_x if couple_x is None else couple_x + base_x
                couple_z = base_z if couple_z is None else couple_z + base_z
                carried = stream * slope_x + across * slope_z + VISCOSITY * curve
                parts.append(adj + STEP_WEIGHT * carried)
            out_ref[0, x, :, cols] = parts[0] - STEP_WEIGHT * couple_x
            out_ref[1, x, :, cols] = parts[1]
            out_ref[2, x, :, cols] = parts[2] - STEP_WEIGHT * couple_z
        return carry

    lax.fori_loop(WIDTH, cells - WIDTH, derive, 0)

    to_right.wait()
    to_left.wait()

    def widen(k, carry):
        ext[:, pl.ds(k, 1)] = halo[0, :, pl.ds(k, 1)].astype(jnp.float32)
        ext[:, pl.ds(k + WIDTH + cells, 1)] = halo[1, :, pl.ds(k, 1)].astype(jnp.float32)
        return carry

    lax.fori_loop(0, WIDTH, widen, 0)

    def edge(k, carry):
        derive(k, 0)
        derive(k + cells - WIDTH, 0)
        return carry

    lax.fori_loop(0, WIDTH, edge, 0)

    loads[2].wait()
    loads[3].wait()

    tall = 6 * step * span
    contract = (((1,), (1,)), ((), ()))

    def wall(c, carry):
        own_copy(c).wait()
        for d in order:
            line_copy(c, d).wait_recv()
        for d in order + [0]:
            block = pl.ds(pl.multiple_of(peers[d] * rows, rows), rows)
            every = lines[c].reshape(tall, groups * rows)
            slopes = lax.dot_general(
                every, first[block, :], contract, preferred_element_type=jnp.float32
            ).reshape(6, step, span, rows)
            curves = lax.dot_general(
                every[tall // 2 :], second[block, :], contract, preferred_element_type=jnp.float32
            ).reshape(3, step, span, rows)
            there = lines[c, :, :, :, block].astype(jnp.float32)
            couple = there[3] * slopes[0] + there[4] * slopes[1] + there[5] * slopes[2]
            parts = [there[1] * slopes[3 + j] + VISCOSITY * curves[j] for j in range(3)]
            parts[1] = parts[1] - couple
            for j in range(3):
                value = parts[j].astype(jnp.bfloat16)
                if d == 0:
                    back_in[c, me, j] = value
                else:
                    back_out[c, d, j] = value
            if d != 0:
                back_copy(c, d).start()
        return carry

    lax.fori_loop(0, chunks, wall, 0)

    place = me * rows + lax.broadcasted_iota(jnp.int32, (span, rows), 1)
    inside = (place > 0) & (place < groups * rows - 1)

    def finish(c, carry):
        for d in order:
            back_copy(c, d).wait_recv()

        def add(t, carry):
            owner = t // step
            within = lax.rem(t, step)
            x = owner * share + c * step + within
            for j in range(3):
                value = out_ref[j, x] + STEP_WEIGHT * back_in[c, owner, j, within].astype(
                    jnp.float32
                )
                out_ref[j, x] = jnp.where(inside, value, 0.0)
            return carry

        return lax.fori_loop(0, groups * step, add, carry)

    lax.fori_loop(0, chunks, finish, 0)

    for c in range(chunks):
        for d in order:
            line_copy(c, d).wait_send()
            back_copy(c, d).wait_send()


def body(base_flow, adjoint, first_op, second_op):
    _, cells, span, rows = base_flow.shape
    groups = lax.axis_size("gy")
    ring = lax.axis_size("gx")
    share = cells // groups
    chunks = 3 if share % 3 == 0 else 1
    step = share // chunks
    total = groups * rows
    low = jnp.bfloat16
    dma = pltpu.SemaphoreType.DMA
    return pl.pallas_call(
        functools.partial(kernel, groups, ring, chunks),
        out_shape=jax.ShapeDtypeStruct(base_flow.shape, jnp.float32),
        in_specs=[pl.BlockSpec(memory_space=pl.ANY)] * 4,
        out_specs=pl.BlockSpec(memory_space=pltpu.VMEM),
        scratch_shapes=[
            pltpu.VMEM((6, cells + 2 * WIDTH, span, rows), jnp.float32),
            pltpu.VMEM((6, cells, span, rows), low),
            pltpu.VMEM((chunks, 6, step, span, total), low),
            pltpu.VMEM((2, 6, WIDTH, span, rows), low),
            pltpu.VMEM((total, total), low),
            pltpu.VMEM((total, total), low),
            pltpu.VMEM((chunks, groups, 3, step, span, rows), low),
            pltpu.VMEM((chunks, groups, 3, step, span, rows), low),
            dma((4,)),
            dma((chunks,)),
            dma((2,)),
            dma((2,)),
            dma((chunks, groups)),
            dma((chunks, groups)),
            dma((chunks, groups)),
            dma((chunks, groups)),
        ],
        compiler_params=pltpu.CompilerParams(
            collective_id=0, has_side_effects=True, vmem_limit_bytes=56 * 1024 * 1024
        ),
    )(base_flow, adjoint, first_op, second_op)


def solution(mesh):
    return jax.shard_map(
        body,
        mesh=mesh,
        in_specs=(P(None, "gx", None, "gy"), P(None, "gx", None, "gy"), P(), P()),
        out_specs=P(None, "gx", None, "gy"),
        check_vma=False,
    )
```

time: 134 us -> 50.9 us (0.38)
  local copies, waits for them, and re-layouts: 55.4 us -> 3.36 us
  Pallas kernels: 0 us -> 46.9 us
  other arithmetic: 33.4 us -> 0 us
  starting transfers between devices: 23.3 us -> 0 us
  waiting for transfers between devices: 13.5 us -> 0 us
  matrix products: 6.92 us -> 0 us
    pallas_call x0 -> x1, Pallas kernels: none -> 46.9 us  [body(): pl.pallas_call(functools.partial(kernel, groups, ring, chunks), out_shape...]
    slice x19 -> x0, local copies, waits for them, and re-layouts: 22.2 us -> none  [the longest x6 10.8 us: first_periodic(): jnp.roll(field, -offset, direction) - jnp.roll(field, offset, direction)]
    add x2 -> x0, other arithmetic: 16.1 us -> none  [the longest x1 15.3 us: body(): base_flow[0][None] * dx_adj + base_flow[2][None] * dz_adj]
    all_to_all x3 -> x0, waiting for transfers between devices: 13.5 us -> none  [the longest x1 11.7 us: body(): lax.all_to_all(wall_part.reshape(wall_part.shape[0], wall_part.shape[1],...]
    all_to_all x3 -> x0, starting transfers between devices: 12.6 us -> none  [the longest x1 4.63 us: body(): lax.all_to_all(wall_part.reshape(wall_part.shape[0], wall_part.shape[1],...]
    unnamed x28 -> x1, local copies, waits for them, and re-layouts: 15 us -> 3.36 us
    reduce_sum x2 -> x0, other arithmetic: 11.2 us -> none  [the longest x1 6.63 us: body(): first_coupling = jnp.sum(adjoint * dx_base, axis=0)]
    ppermute x4 -> x0, starting transfers between devices: 10.7 us -> none  [the longest x2 7.76 us: padded(): lax.ppermute(head, axis, [((i + 1) % count, i) for i in range(count)])]
  transfers between devices with their start and end apart: 7 -> 0, of which waited for: 2 -> 0; matrix products, arithmetic and copies ran while one was open for 58% -> 0% of each run, Pallas kernels for 0% -> 0%
where the time goes in v1:
time: 50.9 us; the launch traced here: 50.3 us
  Pallas kernels  46.9 us (92%)
  local copies, waits for them, and re-layouts  3.36 us (7%)
    pallas_call x1, Pallas kernels, body(): pl.pallas_call(functools.partial(kernel, groups, ring, chunks), out_shape...  46.9 us
    unnamed x1, local copies, waits for them, and re-layouts  3.36 us

profile of v1, /device:TPU:0, one launch (start us, length us, event | category | flops | bytes accessed | tf_op | source)
XLA Modules:
  0.0 50.3 jit_solution(10735255801035619799)
XLA Ops:
  0.0 46.9 %shard_map.46 = f32[3,24,32,256]{3,2,1,0:T(8,128)} custom-call(f32[3,24,32,256]{3,2,1,0:T(8,128)} %base_hbm.1, f32[3,24,32,256]{3,2,1,0:T(8,128)} %adjoint_hbm.1, bf16[1024,1024]{1,0:T(8,128)(2,1)} %first_hbm.1, bf16[1024,1024]{1,0:T(8,128)(2,1)} %second_hbm.1), custom_call_target="tpu_custom_call" | custom-call | tf_op jit(solution)/shard_map/pallas_call | solution.py:274
  46.9 3.4 %copy.6 = f32[3,24,32,256]{3,2,1,0:T(8,128)} copy(f32[3,24,32,256]{3,2,1,0:T(8,128)} %shard_map.46) | data formatting | bytes 4718592

commit v2 on v1

v2 whole, which is shorter than its diff:
```python
import functools

import jax
import jax.numpy as jnp
from jax import lax
from jax.experimental import pallas as pl
from jax.experimental.pallas import tpu as pltpu
from jax.sharding import PartitionSpec as P

C_FIRST = (0.8, -0.2, 4.0 / 105.0, -1.0 / 280.0)
C_SECOND = (1.6, -0.2, 8.0 / 315.0, -1.0 / 560.0)
C_CENTER = -205.0 / 72.0
VISCOSITY = 0.1
STEP_WEIGHT = 0.5
MESH = pl.DeviceIdType.MESH
WIDTH = 4
LANES = 128


def kernel(
    groups,
    ring,
    base_hbm,
    adjoint_hbm,
    first_hbm,
    second_hbm,
    out_ref,
    ext,
    low,
    lines,
    base_lines,
    halo,
    first,
    second,
    chip_first,
    part_out,
    part_in,
    in_sem,
    own_sem,
    halo_send,
    halo_recv,
    line_send,
    line_recv,
):
    cells, span, rows = low.shape[1], low.shape[2], low.shape[3]
    step = WIDTH
    chunks = cells // step
    me = lax.axis_index("gy")
    here = lax.axis_index("gx")
    right = lax.rem(here + 1, ring)
    left = lax.rem(here + ring - 1, ring)
    core = lax.rem(me, 2)
    chip = me // 2
    sibling = me + 1 - 2 * core
    partner = lax.rem(me + 2, groups)

    def block_of(index, size):
        return pl.ds(pl.multiple_of(index * size, size), size)

    mine = block_of(me, rows)
    across_y = block_of(partner, rows)
    chip_columns = block_of(chip, 2 * rows)
    core_columns = block_of(core, rows)
    loads = [
        pltpu.make_async_copy(adjoint_hbm, ext.at[3:6, WIDTH : WIDTH + cells], in_sem.at[0]),
        pltpu.make_async_copy(base_hbm, ext.at[0:3, WIDTH : WIDTH + cells], in_sem.at[1]),
        pltpu.make_async_copy(first_hbm.at[mine], first, in_sem.at[2]),
        pltpu.make_async_copy(second_hbm.at[mine], second, in_sem.at[3]),
        pltpu.make_async_copy(
            first_hbm.at[mine, chip_columns], chip_first.at[0], in_sem.at[4]
        ),
        pltpu.make_async_copy(
            first_hbm.at[across_y, chip_columns], chip_first.at[1], in_sem.at[5]
        ),
    ]
    loads[0].start()
    barrier = pltpu.get_barrier_semaphore()
    for other in (partner, sibling):
        pl.semaphore_signal(barrier, inc=1, device_id={"gy": other}, device_id_type=MESH)
    for side in (left, right):
        pl.semaphore_signal(barrier, inc=1, device_id={"gx": side}, device_id_type=MESH)
    for load in loads[1:]:
        load.start()

    def remote(src, dst, kind, q, axis, target):
        return pltpu.make_async_remote_copy(
            src_ref=src,
            dst_ref=dst,
            send_sem=line_send.at[kind, q],
            recv_sem=line_recv.at[kind, q],
            device_id={axis: target},
            device_id_type=MESH,
        )

    def layers(q):
        return pl.ds(q * step, step)

    def to_partner(q):
        return remote(
            low.at[3:6, layers(q)], lines.at[:, layers(q), :, mine], 0, q, "gy", partner
        )

    def to_sibling(q):
        return remote(
            low.at[3:6, layers(q)], lines.at[:, layers(q), :, mine], 1, q, "gy", sibling
        )

    def base_to_sibling(q):
        return remote(
            low.at[0:3, layers(q)],
            base_lines.at[:, layers(q), :, core_columns],
            2,
            q,
            "gy",
            sibling,
        )

    def forward(q):
        block = lines.at[:, layers(q), :, across_y]
        return remote(block, block, 3, q, "gy", sibling)

    def part_copy(q):
        return remote(part_out.at[layers(q)], part_in.at[layers(q)], 4, q, "gy", partner)

    own_adjoint = pltpu.make_async_copy(low.at[3:6], lines.at[:, :, :, mine], own_sem.at[0])
    own_base = pltpu.make_async_copy(
        low.at[0:3], base_lines.at[:, :, :, core_columns], own_sem.at[1]
    )
    to_right = pltpu.make_async_remote_copy(
        src_ref=low.at[:, cells - WIDTH : cells],
        dst_ref=halo.at[0],
        send_sem=halo_send.at[0],
        recv_sem=halo_recv.at[0],
        device_id={"gx": right},
        device_id_type=MESH,
    )
    to_left = pltpu.make_async_remote_copy(
        src_ref=low.at[:, 0:WIDTH],
        dst_ref=halo.at[1],
        send_sem=halo_send.at[1],
        recv_sem=halo_recv.at[1],
        device_id={"gx": left},
        device_id_type=MESH,
    )
    order = list(range(1, chunks - 1)) + [0, chunks - 1]

    def cast(field, x):
        low[field : field + 3, pl.ds(x, 1)] = ext[
            field : field + 3, pl.ds(x + WIDTH, 1)
        ].astype(jnp.bfloat16)

    def cast_adjoint(x, carry):
        cast(3, x)
        return carry

    def cast_base(x, carry):
        cast(0, x)
        return carry

    loads[0].wait()
    first_step = order[0] * step
    lax.fori_loop(first_step, first_step + step, cast_adjoint, 0)
    pl.semaphore_wait(barrier, 4)
    to_partner(order[0]).start()
    lax.fori_loop(first_step + step, cells, cast_adjoint, 0)
    lax.fori_loop(0, first_step, cast_adjoint, 0)
    for q in order[1:]:
        to_partner(q).start()
    loads[1].wait()
    lax.fori_loop(0, cells, cast_base, 0)
    to_right.start()
    to_left.start()
    for q in order:
        to_sibling(q).start()
        base_to_sibling(q).start()
    own_adjoint.start()
    own_base.start()

    def derive(x, carry):
        for half in range(rows // LANES):
            cols = slice(half * LANES, (half + 1) * LANES)

            def plane(f, offset):
                return ext[f, x + (WIDTH + offset), :, cols]

            stream = plane(0, 0)
            across = plane(2, 0)
            couple_x = None
            couple_z = None
            parts = []
            for j in range(3):
                adj = plane(3 + j, 0)
                slope_x = None
                curve = (2.0 * C_CENTER) * adj
                slope_z = None
                base_x = None
                base_z = None
                field = plane(j, 0)
                for k in range(1, WIDTH + 1):
                    a_up, a_down = plane(3 + j, k), plane(3 + j, -k)
                    z_up = pltpu.roll(adj, span - k, 0)
                    z_down = pltpu.roll(adj, k, 0)
                    dx = C_FIRST[k - 1] * (a_up - a_down)
                    dz = C_FIRST[k - 1] * (z_up - z_down)
                    curve = curve + C_SECOND[k - 1] * ((a_up + a_down) + (z_up + z_down))
                    bx = C_FIRST[k - 1] * (plane(j, k) - plane(j, -k))
                    bz = C_FIRST[k - 1] * (
                        pltpu.roll(field, span - k, 0) - pltpu.roll(field, k, 0)
                    )
                    slope_x = dx if slope_x is None else slope_x + dx
                    slope_z = dz if slope_z is None else slope_z + dz
                    base_x = bx if base_x is None else base_x + bx
                    base_z = bz if base_z is None else base_z + bz
                base_x, base_z = adj * base_x, adj * base_z
                couple_x = base_x if couple_x is None else couple_x + base_x
                couple_z = base_z if couple_z is None else couple_z + base_z
                carried = stream * slope_x + across * slope_z + VISCOSITY * curve
                parts.append(adj + STEP_WEIGHT * carried)
            out_ref[0, x, :, cols] = parts[0] - STEP_WEIGHT * couple_x
            out_ref[1, x, :, cols] = parts[1]
            out_ref[2, x, :, cols] = parts[2] - STEP_WEIGHT * couple_z
        return carry

    tall = 3 * step * span
    contract = (((1,), (1,)), ((), ()))

    def product(values, matrix):
        return lax.dot_general(
            values.reshape(tall, values.shape[3]),
            matrix,
            contract,
            preferred_element_type=jnp.float32,
        ).reshape(3, step, span, rows)

    def couple(q, cols, which):
        slopes = product(base_lines[:, layers(q)], chip_first[which])
        there = lines[:, layers(q), :, cols].astype(jnp.float32)
        return there[0] * slopes[0] + there[1] * slopes[1] + there[2] * slopes[2]

    def advance(q):
        lax.fori_loop(q * step, q * step + step, derive, 0)
        base_to_sibling(q).wait_recv()
        to_partner(q).wait_recv()
        forward(q).start()
        part_out[layers(q)] = couple(q, across_y, 1).astype(jnp.bfloat16)
        part_copy(q).start()

    place = me * rows + lax.broadcasted_iota(jnp.int32, (step, span, rows), 2)
    inside = (place > 0) & (place < groups * rows - 1)

    def wall(q):
        to_sibling(q).wait_recv()
        forward(q).wait_recv()
        here_x = layers(q)
        slopes = product(lines[:, here_x], first[...])
        curves = product(lines[:, here_x], second[...])
        normal = low[1, here_x].astype(jnp.float32)
        own = couple(q, mine, 0)
        for j in range(3):
            part = normal * slopes[j] + VISCOSITY * curves[j]
            if j == 1:
                part = part - own
            value = out_ref[j, here_x] + STEP_WEIGHT * part
            out_ref[j, here_x] = value if j == 1 else jnp.where(inside, value, 0.0)

    def finish(q, carry):
        part_copy(q).wait_recv()
        value = out_ref[1, layers(q)] - STEP_WEIGHT * part_in[layers(q)].astype(jnp.float32)
        out_ref[1, layers(q)] = jnp.where(inside, value, 0.0)
        return carry

    for load in loads[2:]:
        load.wait()
    own_adjoint.wait()
    own_base.wait()
    advance(1)

    def interior(q, carry):
        advance(q)
        wall(q - 1)
        return carry

    lax.fori_loop(2, chunks - 1, interior, 0)

    to_right.wait()
    to_left.wait()

    def widen(k, carry):
        ext[:, pl.ds(k, 1)] = halo[0, :, pl.ds(k, 1)].astype(jnp.float32)
        ext[:, pl.ds(k + WIDTH + cells, 1)] = halo[1, :, pl.ds(k, 1)].astype(jnp.float32)
        return carry

    lax.fori_loop(0, WIDTH, widen, 0)

    def edges(k, carry):
        q = k * (chunks - 1)
        advance(q)
        wall((1 - k) * (chunks - 2))
        return carry

    lax.fori_loop(0, 2, edges, 0)
    wall(chunks - 1)
    lax.fori_loop(0, chunks, finish, 0)

    for q in range(chunks):
        for copy in (to_partner, to_sibling, base_to_sibling, forward, part_copy):
            copy(q).wait_send()


def body(base_flow, adjoint, first_op, second_op):
    _, cells, span, rows = base_flow.shape
    groups = lax.axis_size("gy")
    ring = lax.axis_size("gx")
    chunks = cells // WIDTH
    total = groups * rows
    low = jnp.bfloat16
    dma = pltpu.SemaphoreType.DMA
    return pl.pallas_call(
        functools.partial(kernel, groups, ring),
        out_shape=jax.ShapeDtypeStruct(base_flow.shape, jnp.float32),
        in_specs=[pl.BlockSpec(memory_space=pltpu.HBM)] * 4,
        out_specs=pl.BlockSpec(memory_space=pltpu.VMEM),
        scratch_shapes=[
            pltpu.VMEM((6, cells + 2 * WIDTH, span, rows), jnp.float32),
            pltpu.VMEM((6, cells, span, rows), low),
            pltpu.VMEM((3, cells, span, total), low),
            pltpu.VMEM((3, cells, span, 2 * rows), low),
            pltpu.VMEM((2, 6, WIDTH, span, rows), low),
            pltpu.VMEM((rows, total), low),
            pltpu.VMEM((rows, total), low),
            pltpu.VMEM((2, rows, 2 * rows), low),
            pltpu.VMEM((cells, span, rows), low),
            pltpu.VMEM((cells, span, rows), low),
            dma((6,)),
            dma((2,)),
            dma((2,)),
            dma((2,)),
            dma((5, chunks)),
            dma((5, chunks)),
        ],
        compiler_params=pltpu.CompilerParams(
            collective_id=0, has_side_effects=True, vmem_limit_bytes=54 * 1024 * 1024
        ),
    )(base_flow, adjoint, first_op, second_op)


def solution(mesh):
    return jax.shard_map(
        body,
        mesh=mesh,
        in_specs=(P(None, "gx", None, "gy"), P(None, "gx", None, "gy"), P(), P()),
        out_specs=P(None, "gx", None, "gy"),
        check_vma=False,
    )
```

time: 50.9 us -> 47.2 us (0.927)
  Pallas kernels: 46.9 us -> 43.7 us
    pallas_call x1, Pallas kernels: 46.9 us -> 43.7 us  [body(): pl.pallas_call(functools.partial(kernel, groups, ring), out_shape=jax.Sha...]
where the time goes in v2:
time: 47.2 us; the launch traced here: 47.1 us
  Pallas kernels  43.7 us (93%)
  local copies, waits for them, and re-layouts  3.36 us (7%)
    pallas_call x1, Pallas kernels, body(): pl.pallas_call(functools.partial(kernel, groups, ring), out_shape=jax.Sha...  43.7 us
    unnamed x1, local copies, waits for them, and re-layouts  3.36 us

profile of v2, /device:TPU:0, one launch (start us, length us, event | category | flops | bytes accessed | tf_op | source)
XLA Modules:
  0.0 47.1 jit_solution(1463448304989852695)
XLA Ops:
  0.0 43.7 %shard_map.46 = f32[3,24,32,256]{3,2,1,0:T(8,128)} custom-call(f32[3,24,32,256]{3,2,1,0:T(8,128)} %base_hbm.1, f32[3,24,32,256]{3,2,1,0:T(8,128)} %adjoint_hbm.1, bf16[1024,1024]{1,0:T(8,128)(2,1)} %first_hbm.1, bf16[1024,1024]{1,0:T(8,128)(2,1)} %second_hbm.1), custom_call_target="tpu_custom_call" | custom-call | tf_op jit(solution)/shard_map/pallas_call | solution.py:318
  43.7 3.4 %copy.6 = f32[3,24,32,256]{3,2,1,0:T(8,128)} copy(f32[3,24,32,256]{3,2,1,0:T(8,128)} %shard_map.46) | data formatting | bytes 4718592

commit v3 on v2

--- a/solution.py
+++ b/solution.py
@@ -24,6 +24,7 @@
     adjoint_hbm,
     first_hbm,
     second_hbm,
+    out_hbm,
     out_ref,
     ext,
     low,
@@ -36,6 +37,7 @@
     part_out,
     part_in,
     in_sem,
+    out_sem,
     own_sem,
     halo_send,
     halo_recv,
@@ -61,26 +63,33 @@
     across_y = block_of(partner, rows)
     chip_columns = block_of(chip, 2 * rows)
     core_columns = block_of(core, rows)
+    order = list(range(1, chunks - 1)) + [0, chunks - 1]
+    adjoint_loads = [
+        pltpu.make_async_copy(
+            adjoint_hbm.at[:, q * step : (q + 1) * step],
+            ext.at[3:6, WIDTH + q * step : WIDTH + (q + 1) * step],
+            in_sem.at[5 + q],
+        )
+        for q in range(chunks)
+    ]
     loads = [
-        pltpu.make_async_copy(adjoint_hbm, ext.at[3:6, WIDTH : WIDTH + cells], in_sem.at[0]),
-        pltpu.make_async_copy(base_hbm, ext.at[0:3, WIDTH : WIDTH + cells], in_sem.at[1]),
-        pltpu.make_async_copy(first_hbm.at[mine], first, in_sem.at[2]),
-        pltpu.make_async_copy(second_hbm.at[mine], second, in_sem.at[3]),
+        pltpu.make_async_copy(base_hbm, ext.at[0:3, WIDTH : WIDTH + cells], in_sem.at[0]),
+        pltpu.make_async_copy(first_hbm.at[mine], first, in_sem.at[1]),
+        pltpu.make_async_copy(second_hbm.at[mine], second, in_sem.at[2]),
         pltpu.make_async_copy(
-            first_hbm.at[mine, chip_columns], chip_first.at[0], in_sem.at[4]
+            first_hbm.at[mine, chip_columns], chip_first.at[0], in_sem.at[3]
         ),
         pltpu.make_async_copy(
-            first_hbm.at[across_y, chip_columns], chip_first.at[1], in_sem.at[5]
+            first_hbm.at[across_y, chip_columns], chip_first.at[1], in_sem.at[4]
         ),
     ]
-    loads[0].start()
     barrier = pltpu.get_barrier_semaphore()
     for other in (partner, sibling):
         pl.semaphore_signal(barrier, inc=1, device_id={"gy": other}, device_id_type=MESH)
     for side in (left, right):
         pl.semaphore_signal(barrier, inc=1, device_id={"gx": side}, device_id_type=MESH)
-    for load in loads[1:]:
-        load.start()
+    for q in order:
+        adjoint_loads[q].start()
 
     def remote(src, dst, kind, q, axis, target):
         return pltpu.make_async_remote_copy(
@@ -142,8 +151,6 @@
         device_id={"gx": left},
         device_id_type=MESH,
     )
-    order = list(range(1, chunks - 1)) + [0, chunks - 1]
-
     def cast(field, x):
         low[field : field + 3, pl.ds(x, 1)] = ext[
             field : field + 3, pl.ds(x + WIDTH, 1)
@@ -157,16 +164,15 @@
         cast(0, x)
         return carry
 
+    for q in order:
+        adjoint_loads[q].wait()
+        lax.fori_loop(q * step, (q + 1) * step, cast_adjoint, 0)
+        if q == order[0]:
+            pl.semaphore_wait(barrier, 4)
+            for load in loads:
+                load.start()
+        to_partner(q).start()
     loads[0].wait()
-    first_step = order[0] * step
-    lax.fori_loop(first_step, first_step + step, cast_adjoint, 0)
-    pl.semaphore_wait(barrier, 4)
-    to_partner(order[0]).start()
-    lax.fori_loop(first_step + step, cells, cast_adjoint, 0)
-    lax.fori_loop(0, first_step, cast_adjoint, 0)
-    for q in order[1:]:
-        to_partner(q).start()
-    loads[1].wait()
     lax.fori_loop(0, cells, cast_base, 0)
     to_right.start()
     to_left.start()
@@ -245,6 +251,11 @@
         part_out[layers(q)] = couple(q, across_y, 1).astype(jnp.bfloat16)
         part_copy(q).start()
 
+    def store(j, q):
+        return pltpu.make_async_copy(
+            out_ref.at[j, layers(q)], out_hbm.at[j, layers(q)], out_sem.at[j, q]
+        )
+
     place = me * rows + lax.broadcasted_iota(jnp.int32, (step, span, rows), 2)
     inside = (place > 0) & (place < groups * rows - 1)
 
@@ -262,14 +273,17 @@
                 part = part - own
             value = out_ref[j, here_x] + STEP_WEIGHT * part
             out_ref[j, here_x] = value if j == 1 else jnp.where(inside, value, 0.0)
+            if j != 1:
+                store(j, q).start()
 
     def finish(q, carry):
         part_copy(q).wait_recv()
         value = out_ref[1, layers(q)] - STEP_WEIGHT * part_in[layers(q)].astype(jnp.float32)
         out_ref[1, layers(q)] = jnp.where(inside, value, 0.0)
-        return carry
-
-    for load in loads[2:]:
+        store(1, q).start()
+        return carry
+
+    for load in loads[1:]:
         load.wait()
     own_adjoint.wait()
     own_base.wait()
@@ -299,12 +313,37 @@
         return carry
 
     lax.fori_loop(0, 2, edges, 0)
+    lax.fori_loop(1, chunks - 1, finish, 0)
     wall(chunks - 1)
-    lax.fori_loop(0, chunks, finish, 0)
+    finish(0, 0)
+    finish(chunks - 1, 0)
 
     for q in range(chunks):
         for copy in (to_partner, to_sibling, base_to_sibling, forward, part_copy):
             copy(q).wait_send()
+        for j in range(3):
+            store(j, q).wait()
+
+
+def hand_on(source, target, held, sems):
+    half = source.shape[1] // 2
+    pieces = []
+    for j in range(3):
+        for h in range(2):
+            part = pl.ds(h * half, half)
+            pieces.append(
+                (
+                    pltpu.make_async_copy(source.at[j, part], held.at[j, part], sems.at[0, j, h]),
+                    pltpu.make_async_copy(held.at[j, part], target.at[j, part], sems.at[1, j, h]),
+                )
+            )
+    for arrive, _ in pieces:
+        arrive.start()
+    for arrive, leave in pieces:
+        arrive.wait()
+        leave.start()
+    for _, leave in pieces:
+        leave.wait()
 
 
 def body(base_flow, adjoint, first_op, second_op):
@@ -315,12 +354,13 @@
     total = groups * rows
     low = jnp.bfloat16
     dma = pltpu.SemaphoreType.DMA
-    return pl.pallas_call(
+    updated = pl.pallas_call(
         functools.partial(kernel, groups, ring),
         out_shape=jax.ShapeDtypeStruct(base_flow.shape, jnp.float32),
         in_specs=[pl.BlockSpec(memory_space=pltpu.HBM)] * 4,
-        out_specs=pl.BlockSpec(memory_space=pltpu.VMEM),
+        out_specs=pl.BlockSpec(memory_space=pltpu.HBM),
         scratch_shapes=[
+            pltpu.VMEM((3, cells, span, rows), jnp.float32),
             pltpu.VMEM((6, cells + 2 * WIDTH, span, rows), jnp.float32),
             pltpu.VMEM((6, cells, span, rows), low),
             pltpu.VMEM((3, cells, span, total), low),
@@ -331,7 +371,8 @@
             pltpu.VMEM((2, rows, 2 * rows), low),
             pltpu.VMEM((cells, span, rows), low),
             pltpu.VMEM((cells, span, rows), low),
-            dma((6,)),
+            dma((5 + chunks,)),
+            dma((3, chunks)),
             dma((2,)),
             dma((2,)),
             dma((2,)),
@@ -342,6 +383,13 @@
             collective_id=0, has_side_effects=True, vmem_limit_bytes=54 * 1024 * 1024
         ),
     )(base_flow, adjoint, first_op, second_op)
+    return pl.pallas_call(
+        hand_on,
+        out_shape=jax.ShapeDtypeStruct(base_flow.shape, jnp.float32),
+        in_specs=[pl.BlockSpec(memory_space=pltpu.HBM)],
+        out_specs=pl.BlockSpec(memory_space=pltpu.HBM),
+        scratch_shapes=[pltpu.VMEM(base_flow.shape, jnp.float32), dma((2, 3, 2))],
+    )(updated)
 
 
 def solution(mesh):

time: 47.2 us -> 45.8 us (0.970)
  local copies, waits for them, and re-layouts: 3.36 us -> 0 us
  Pallas kernels: 43.7 us -> 45.6 us
    unnamed x1 -> x0, local copies, waits for them, and re-layouts: 3.36 us -> none
    pallas_call x0 -> x1, Pallas kernels: none -> 2.49 us  [body(): pl.pallas_call(hand_on, out_shape=jax.ShapeDtypeStruct(base_flow.shape, j...]
    pallas_call x1, Pallas kernels: 43.7 us -> 43.1 us  [body(): pl.pallas_call(functools.partial(kernel, groups, ring), out_shape=jax.Sha...]
where the time goes in v3:
time: 45.8 us; the launch traced here: 45.6 us
  Pallas kernels  45.6 us (100%)
    pallas_call x1, Pallas kernels, body(): pl.pallas_call(functools.partial(kernel, groups, ring), out_shape=jax.Sha...  43.1 us
    pallas_call x1, Pallas kernels, body(): pl.pallas_call(hand_on, out_shape=jax.ShapeDtypeStruct(base_flow.shape, j...  2.49 us

profile of v3, /device:TPU:0, one launch (start us, length us, event | category | flops | bytes accessed | tf_op | source)
XLA Modules:
  0.0 45.6 jit_solution(2302039517438166161)
XLA Ops:
  0.0 43.1 %shard_map.46.source = f32[3,24,32,256]{3,2,1,0:T(8,128)} custom-call(f32[3,24,32,256]{3,2,1,0:T(8,128)} %base_hbm.1, f32[3,24,32,256]{3,2,1,0:T(8,128)} %adjoint_hbm.1, bf16[1024,1024]{1,0:T(8,128)(2,1)} %first_hbm.1, bf16[1024,1024]{1,0:T(8,128)(2,1)} %second_hbm.1), custom_call_target="tpu_custom_call" | custom-call | tf_op jit(solution)/shard_map/pallas_call | solution.py:357
  43.1 2.5 %shard_map.47 = f32[3,24,32,256]{3,2,1,0:T(8,128)} custom-call(f32[3,24,32,256]{3,2,1,0:T(8,128)} %shard_map.46.source), custom_call_target="tpu_custom_call" | custom-call | tf_op jit(solution)/shard_map/pallas_call | solution.py:386
